TPU v7x, 256 devices: a whole 4x4x8 slice. The times are simulated.
256 devices in a mesh: dp: 64 (over z, y, x_lo), mp: 4 (over x_hi, core).
Axes of the slice: x: 4 (x_hi: 2, x_lo: 2; x = x_hi * 2 + x_lo), y: 4, z: 8, core: 2. Of those that a mesh axis runs over, the one named last changes fastest.
Arguments:
- tokens: bfloat16 [18432, 5120], P(('dp', 'mp')), may hold values from -24 to 24
- gate_weight: bfloat16 [5120, 8704], P('dp', 'mp'), may hold values from -0.078125 to 0.078125
- grad_hidden: bfloat16 [8192, 8704], P('dp', 'mp'), may hold values from -16 to 16
- counts: int32 [64], P('dp'), may hold values from 1 to 288, 6144 in all
- sampled: int32 [8192], P('dp'), may hold values from 0 to 287
- owner_map: int32 [64], replicated, may hold values from 0 to 63, each once
- input_factor: float32 [4, 1280, 128], P('mp', 'dp'), may hold values from -3 to 3
- grad_factor: float32 [4, 2176, 128], P('mp', 'dp'), may hold values from -3 to 3
Outputs:
- activation: bfloat16 [18432, 8704], P('dp', 'mp')
- input_ema: float32 [4, 1280, 128], P('mp', 'dp')
- grad_ema: float32 [4, 2176, 128], P('mp', 'dp')
Inputs may be any that keep to these rules, and one draw needn't show every extreme that they name: The largest count is 288; the sum of the counts differs between draws. `sampled`: positions may lie past their group's count. `owner_map`: each rank once.
All inputs are finite; a program needn't handle non-finite values. No bound on the sum of `counts` on one device may be relied on, other than what follows from the above.
Results may differ from a plain program's by a relative error of at most 0.0014.
Values may be sent and summed in bfloat16 or wider, within the bound.
No kernel may reach another device: no remote copies, remote signals or barrier semaphores. Data moves between devices by JAX's collectives and lax.ppermute only.
A program may use at most 128 MiB of HBM per device.

v0:
```python
import jax
import jax.numpy as jnp
from jax import lax
from jax.sharding import PartitionSpec as P

EMA_DECAY = 0.8


def stacked_grams(matrix_rows, blk_size):
    stacked = matrix_rows.reshape(matrix_rows.shape[0], -1, blk_size)
    grams = jnp.einsum("tkb,tkc->kbc", stacked, stacked, preferred_element_type=jnp.float32)
    return grams.reshape(-1, blk_size)


def local(tokens, gate_weight, grad_hidden, counts, sampled, owner_map, input_factor, grad_factor):
    n_dp = lax.axis_size("dp")
    n_mp = lax.axis_size("mp")
    mp_index = lax.axis_index("mp")
    feat_width = tokens.shape[1]
    blk_size = input_factor.shape[2]
    group = lax.all_gather(tokens, "mp", axis=0, tiled=True)
    tok_dev = group.shape[0]
    own_count = counts[0]
    is_live = lax.iota(jnp.int32, tok_dev) < own_count
    all_tokens = lax.psum(jnp.sum(counts).astype(jnp.float32), "dp")
    gate_sums = jnp.dot(
        group,
        lax.all_gather(gate_weight, "dp", axis=0, tiled=True),
        preferred_element_type=jnp.float32,
    )
    activation = jnp.where(is_live[:, None], jax.nn.silu(gate_sums), 0.0).astype(jnp.bfloat16)

    def arrange(statistic):
        strips = statistic.reshape(n_dp, -1, blk_size)
        return jnp.take(strips, owner_map, axis=0).reshape(statistic.shape)

    masked = jnp.where(is_live[:, None], group, jnp.zeros((), jnp.bfloat16))
    region_rows = feat_width // n_mp
    own_columns = lax.dynamic_slice_in_dim(masked, mp_index * region_rows, region_rows, 1)
    gram_blocks = stacked_grams(own_columns, blk_size)
    input_stat = lax.psum_scatter(arrange(gram_blocks), "dp", scatter_dimension=0, tiled=True)
    input_ema = EMA_DECAY * input_factor + (1.0 - EMA_DECAY) * (input_stat / all_tokens).reshape(
        input_factor.shape
    )
    picked = jnp.take(activation, sampled, axis=0)
    grad_rows = (grad_hidden.astype(jnp.float32) * picked.astype(jnp.float32)).astype(jnp.bfloat16)
    grad_blocks_local = stacked_grams(grad_rows, blk_size)
    grad_stat = lax.psum_scatter(arrange(grad_blocks_local), "dp", scatter_dimension=0, tiled=True)
    sample_total = jnp.float32(grad_hidden.shape[0] * n_dp)
    grad_ema = EMA_DECAY * grad_factor + (1.0 - EMA_DECAY) * (grad_stat / sample_total).reshape(
        grad_factor.shape
    )
    return (activation, input_ema, grad_ema)


def solution(mesh):
    in_specs = (
        P(("dp", "mp"), None),
        P("dp", "mp"),
        P("dp", "mp"),
        P("dp"),
        P("dp"),
        P(),
        P("mp", "dp", None),
        P("mp", "dp", None),
    )
    out_specs = (P("dp", "mp"), P("mp", "dp", None), P("mp", "dp", None))
    return jax.shard_map(local, mesh=mesh, in_specs=in_specs, out_specs=out_specs, check_vma=False)
```

profile of v0, /device:TPU:4, one launch (start us, length us, event | category | flops | bytes accessed | tf_op | source)
XLA Modules:
  0.0 1118.9 jit_solution(10709277292369163569)
XLA Ops:
  7.2 0.7 all-gather.3.cloned.1.call-update
  7.9 0.7 all-gather.5.cloned.1.call-update
  9.3 0.7 compare_and_fusion.1
  10.5 0.7 compare_select_fusion
  11.1 0.7 compare_select_fusion.1
  11.8 0.7 compare_and_fusion
  12.5 31.7 %all-gather.3.cloned.1.call-done = bf16[288,5120]{1,0:T(8,128)(2,1)} async-done(((bf16[72,5120]{1,0:T(8,128)(2,1)}), bf16[288,5120]{1,0:T(8,128)(2,1)}) %all-gather.3.cloned.1.call-update) | async-done | bytes 2949136 | tf_op jit(solution)/shard_map/all_gather | solution.py:21
  44.1 1.3 dynamic-slice_select_fusion
  45.4 0.6 copy.23
  46.1 0.5 fusion.7
  46.7 0.6 gather_fusion
  47.4 1.1 broadcast_select_fusion.1
  48.5 486.1 %all-gather.5.cloned.1.call-done = bf16[5120,2176]{1,0:T(8,128)(2,1)} async-done(((bf16[80,2176]{1,0:T(8,128)(2,1)}), bf16[5120,2176]{1,0:T(8,128)(2,1)}) %all-gather.5.cloned.1.call-update) | async-done | bytes 22282256 | tf_op jit(solution)/shard_map/all_gather | solution.py:28
  534.5 13.3 %select_convert_fusion = bf16[288,2176]{1,0:T(8,128)(2,1)S(1)} fusion(pred[288]{0:T(512)(128)(4,1)S(1)} %iota_compare_fusion, bf16[288,5120]{1,0:T(8,128)(2,1)} %all-gather.3.cloned.1.call-done, bf16[5120,2176]{1,0:T(8,128)(2,1)} %all-gather.5.cloned.1.call-done), kind=kOutput, calls=%fused_computation.3 | convolution fusion | flops 6421045248 | bytes 26485024 | tf_op jit(solution)/shard_map/dot_general | solution.py:26
  547.9 1.0 gather_fusion.1
  548.9 0.4 copy-done.1
  549.3 0.2 multiply_convert_fusion
  549.5 0.3 copy.27
  549.9 0.5 fusion.8
  550.5 0.7 gather_fusion.2
  551.3 0.4 broadcast_select_fusion
  551.6 167.2 %fusion = f32[48,128]{1,0:T(8,128)S(1)} fusion(f32[2176,128]{1,0:T(8,128)S(1)} %broadcast_select_fusion), kind=kCustom, calls=%all-reduce-scatter | all-reduce-scatter fusion | flops 393217 | bytes 1139712
  718.9 1.3 collective-permute-start
  720.2 1.3 collective-permute-start.1
  721.5 1.3 collective-permute-start.10
  722.8 13.1 %collective-permute-start.18 = (f32[18,128]{1,0:T(8,128)S(1)}, f32[18,128]{1,0:T(8,128)S(1)}, u32[]{:S(2)}, u32[]{:S(2)}) collective-permute-start(f32[18,128]{1,0:T(8,128)S(1)} %slice.6), channel_id=1, source_target_pairs={{0,76},{4,80},{8,84},{12,88},{16,92},{20,96},{24,100},{28,104},{32... | collective-permute-start | bytes 27656
  735.9 2.5 collective-permute-start.11
  738.5 1.3 collective-permute-start.12
  739.8 1.8 collective-permute-start.13
  741.6 7.7 collective-permute-start.14
  749.3 1.9 collective-permute-start.15
  751.2 3.2 collective-permute-start.16
  754.4 2.8 collective-permute-start.17
  757.2 3.6 collective-permute-start.2
  760.9 3.5 collective-permute-start.3
  764.4 1.6 collective-permute-start.4
  766.0 155.6 %psum.7 = f32[]{:T(128)} all-reduce(f32[]{:T(128)S(6)} %convert_element_type.16), channel_id=1, replica_groups=mesh['dp'=64,'mp'=4] {'dp'}, use_global_device_ids=true, to_apply=%region_1.0 | all-reduce | flops 1 | bytes 8 | tf_op jit(solution)/shard_map/psum | solution.py:25
  921.6 0.6 fusion.6
  923.5 1.3 collective-permute-start.5
  924.8 1.3 collective-permute-start.6
  926.1 1.3 collective-permute-start.7
  927.4 1.3 collective-permute-start.8
  928.7 7.5 collective-permute-start.9
  936.2 170.6 %all-reduce.5.cloned.1.call-done = f32[1280,128]{1,0:T(8,128)} async-done(((f32[1280,128]{1,0:T(8,128)}), f32[1280,128]{1,0:T(8,128)}) %all-reduce.5.cloned.1.call-update) | async-done | bytes 655376
  1106.8 1.4 fusion.5
  1108.2 0.6 copy.29
  1108.8 2.9 concatenate
  1111.8 0.6 copy.30
  (45 shorter events, 1.0 us)
Async XLA Ops:
  7.2 36.9 %all-gather.3.cloned.1.call-start = ((), (), s32[]{:S(2)}) async-start(), calls=%async_computation | async-start | bytes 3686400 | tf_op jit(solution)/shard_map/all_gather | solution.py:21
  7.9 526.6 %all-gather.5.cloned.1.call-start = ((), (), s32[]{:S(2)}) async-start(), calls=%async_computation.1 | async-start | bytes 22630400 | tf_op jit(solution)/shard_map/all_gather | solution.py:28
  8.6 1098.1 %all-reduce.5.cloned.1.call-start = ((), (), s32[]{:S(2)}) async-start(), calls=%async_computation.2 | async-start | bytes 1310720
  547.8 1.0 copy-start
  547.8 1.5 copy-start.1
  551.2 370.4 %copy-start.4 = (u32[256]{0:T(256)S(1)}, u32[256]{0:T(256)}, u32[]{:S(2)}) copy-start(u32[256]{0:T(256)} %constant.76) | copy-start | bytes 3076
  551.2 555.5 %copy-start.3 = (f32[1,20,128]{2,0,1:T(1,128)S(1)}, f32[1,20,128]{2,0,1:T(1,128)}, u32[]{:S(2)}) copy-start(f32[1,20,128]{2,0,1:T(1,128)} %param.14) | copy-start | bytes 30724
  551.6 560.1 %copy-start.2 = (f32[1,34,128]{2,0,1:T(1,128)S(1)}, f32[1,34,128]{2,0,1:T(1,128)}, u32[]{:S(2)}) copy-start(f32[1,34,128]{2,0,1:T(1,128)} %param.15) | copy-start | bytes 52228
  718.9 20.9 %collective-permute-start = (f32[48,128]{1,0:T(8,128)S(1)}, f32[48,128]{1,0:T(8,128)S(1)}, u32[]{:S(2)}, u32[]{:S(2)}) collective-permute-start(f32[48,128]{1,0:T(8,128)S(1)} %fusion), channel_id=1, source_target_pairs={{0,4},{4,8},{8,12},{12,16},{16,20},{20,24},{24,28},{28,32},{32,36}... | collective-permute-start | bytes 73736
  720.2 21.4 %collective-permute-start.1 = (f32[48,128]{1,0:T(8,128)S(1)}, f32[48,128]{1,0:T(8,128)S(1)}, u32[]{:S(2)}, u32[]{:S(2)}) collective-permute-start(f32[48,128]{1,0:T(8,128)S(1)} %fusion), channel_id=1, source_target_pairs={{0,8},{4,12},{8,16},{12,20},{16,24},{20,28},{24,32},{28,36},{32,40... | collective-permute-start | bytes 73736
  721.5 27.8 %collective-permute-start.10 = (f32[48,128]{1,0:T(8,128)S(1)}, f32[48,128]{1,0:T(8,128)S(1)}, u32[]{:S(2)}, u32[]{:S(2)}) collective-permute-start(f32[48,128]{1,0:T(8,128)S(1)} %fusion), channel_id=1, source_target_pairs={{0,44},{4,48},{8,52},{12,56},{16,60},{20,64},{24,68},{28,72},{32,7... | collective-permute-start | bytes 73736
  722.8 15.7 %collective-permute-start.18 = (f32[18,128]{1,0:T(8,128)S(1)}, f32[18,128]{1,0:T(8,128)S(1)}, u32[]{:S(2)}, u32[]{:S(2)}) collective-permute-start(f32[18,128]{1,0:T(8,128)S(1)} %slice.6), channel_id=1, source_target_pairs={{0,76},{4,80},{8,84},{12,88},{16,92},{20,96},{24,100},{28,104},{32... | collective-permute-start | bytes 27656
  735.9 15.3 %collective-permute-start.11 = (f32[48,128]{1,0:T(8,128)S(1)}, f32[48,128]{1,0:T(8,128)S(1)}, u32[]{:S(2)}, u32[]{:S(2)}) collective-permute-start(f32[48,128]{1,0:T(8,128)S(1)} %fusion), channel_id=1, source_target_pairs={{0,48},{4,52},{8,56},{12,60},{16,64},{20,68},{24,72},{28,76},{32,8... | collective-permute-start | bytes 73736
  738.5 15.9 %collective-permute-start.12 = (f32[48,128]{1,0:T(8,128)S(1)}, f32[48,128]{1,0:T(8,128)S(1)}, u32[]{:S(2)}, u32[]{:S(2)}) collective-permute-start(f32[48,128]{1,0:T(8,128)S(1)} %fusion), channel_id=1, source_target_pairs={{0,52},{4,56},{8,60},{12,64},{16,68},{20,72},{24,76},{28,80},{32,8... | collective-permute-start | bytes 73736
  739.8 17.4 %collective-permute-start.13 = (f32[48,128]{1,0:T(8,128)S(1)}, f32[48,128]{1,0:T(8,128)S(1)}, u32[]{:S(2)}, u32[]{:S(2)}) collective-permute-start(f32[48,128]{1,0:T(8,128)S(1)} %fusion), channel_id=1, source_target_pairs={{0,56},{4,60},{8,64},{12,68},{16,72},{20,76},{24,80},{28,84},{32,8... | collective-permute-start | bytes 73736
  741.6 19.3 %collective-permute-start.14 = (f32[48,128]{1,0:T(8,128)S(1)}, f32[48,128]{1,0:T(8,128)S(1)}, u32[]{:S(2)}, u32[]{:S(2)}) collective-permute-start(f32[48,128]{1,0:T(8,128)S(1)} %fusion), channel_id=1, source_target_pairs={{0,60},{4,64},{8,68},{12,72},{16,76},{20,80},{24,84},{28,88},{32,9... | collective-permute-start | bytes 73736
  749.3 15.2 %collective-permute-start.15 = (f32[48,128]{1,0:T(8,128)S(1)}, f32[48,128]{1,0:T(8,128)S(1)}, u32[]{:S(2)}, u32[]{:S(2)}) collective-permute-start(f32[48,128]{1,0:T(8,128)S(1)} %fusion), channel_id=1, source_target_pairs={{0,64},{4,68},{8,72},{12,76},{16,80},{20,84},{24,88},{28,92},{32,9... | collective-permute-start | bytes 73736
  751.2 172.3 %collective-permute-start.16 = (f32[48,128]{1,0:T(8,128)S(1)}, f32[48,128]{1,0:T(8,128)S(1)}, u32[]{:S(2)}, u32[]{:S(2)}) collective-permute-start(f32[48,128]{1,0:T(8,128)S(1)} %fusion), channel_id=1, source_target_pairs={{0,68},{4,72},{8,76},{12,80},{16,84},{20,88},{24,92},{28,96},{32,1... | collective-permute-start | bytes 73736
  754.4 170.4 %collective-permute-start.17 = (f32[48,128]{1,0:T(8,128)S(1)}, f32[48,128]{1,0:T(8,128)S(1)}, u32[]{:S(2)}, u32[]{:S(2)}) collective-permute-start(f32[48,128]{1,0:T(8,128)S(1)} %fusion), channel_id=1, source_target_pairs={{0,72},{4,76},{8,80},{12,84},{16,88},{20,92},{24,96},{28,100},{32,... | collective-permute-start | bytes 73736
  757.2 168.9 %collective-permute-start.2 = (f32[48,128]{1,0:T(8,128)S(1)}, f32[48,128]{1,0:T(8,128)S(1)}, u32[]{:S(2)}, u32[]{:S(2)}) collective-permute-start(f32[48,128]{1,0:T(8,128)S(1)} %fusion), channel_id=1, source_target_pairs={{0,12},{4,16},{8,20},{12,24},{16,28},{20,32},{24,36},{28,40},{32,4... | collective-permute-start | bytes 73736
  760.9 166.5 %collective-permute-start.3 = (f32[48,128]{1,0:T(8,128)S(1)}, f32[48,128]{1,0:T(8,128)S(1)}, u32[]{:S(2)}, u32[]{:S(2)}) collective-permute-start(f32[48,128]{1,0:T(8,128)S(1)} %fusion), channel_id=1, source_target_pairs={{0,16},{4,20},{8,24},{12,28},{16,32},{20,36},{24,40},{28,44},{32,4... | collective-permute-start | bytes 73736
  764.4 164.3 %collective-permute-start.4 = (f32[48,128]{1,0:T(8,128)S(1)}, f32[48,128]{1,0:T(8,128)S(1)}, u32[]{:S(2)}, u32[]{:S(2)}) collective-permute-start(f32[48,128]{1,0:T(8,128)S(1)} %fusion), channel_id=1, source_target_pairs={{0,20},{4,24},{8,28},{12,32},{16,36},{20,40},{24,44},{28,48},{32,5... | collective-permute-start | bytes 73736
  923.5 185.3 %collective-permute-start.5 = (f32[48,128]{1,0:T(8,128)S(1)}, f32[48,128]{1,0:T(8,128)S(1)}, u32[]{:S(2)}, u32[]{:S(2)}) collective-permute-start(f32[48,128]{1,0:T(8,128)S(1)} %fusion), channel_id=1, source_target_pairs={{0,24},{4,28},{8,32},{12,36},{16,40},{20,44},{24,48},{28,52},{32,5... | collective-permute-start | bytes 73736
  924.8 184.0 %collective-permute-start.6 = (f32[48,128]{1,0:T(8,128)S(1)}, f32[48,128]{1,0:T(8,128)S(1)}, u32[]{:S(2)}, u32[]{:S(2)}) collective-permute-start(f32[48,128]{1,0:T(8,128)S(1)} %fusion), channel_id=1, source_target_pairs={{0,28},{4,32},{8,36},{12,40},{16,44},{20,48},{24,52},{28,56},{32,6... | collective-permute-start | bytes 73736
  926.1 182.7 %collective-permute-start.7 = (f32[48,128]{1,0:T(8,128)S(1)}, f32[48,128]{1,0:T(8,128)S(1)}, u32[]{:S(2)}, u32[]{:S(2)}) collective-permute-start(f32[48,128]{1,0:T(8,128)S(1)} %fusion), channel_id=1, source_target_pairs={{0,32},{4,36},{8,40},{12,44},{16,48},{20,52},{24,56},{28,60},{32,6... | collective-permute-start | bytes 73736
  927.4 181.4 %collective-permute-start.8 = (f32[48,128]{1,0:T(8,128)S(1)}, f32[48,128]{1,0:T(8,128)S(1)}, u32[]{:S(2)}, u32[]{:S(2)}) collective-permute-start(f32[48,128]{1,0:T(8,128)S(1)} %fusion), channel_id=1, source_target_pairs={{0,36},{4,40},{8,44},{12,48},{16,52},{20,56},{24,60},{28,64},{32,6... | collective-permute-start | bytes 73736
  928.7 180.1 %collective-permute-start.9 = (f32[48,128]{1,0:T(8,128)S(1)}, f32[48,128]{1,0:T(8,128)S(1)}, u32[]{:S(2)}, u32[]{:S(2)}) collective-permute-start(f32[48,128]{1,0:T(8,128)S(1)} %fusion), channel_id=1, source_target_pairs={{0,40},{4,44},{8,48},{12,52},{16,56},{20,60},{24,64},{28,68},{32,7... | collective-permute-start | bytes 73736
Sparse Core Ops, SparseCore 0:
  9.8 34.2 all-gather.2
  45.9 488.6 all-gather.4
  537.2 569.5 all-reduce.4
where the time goes:
time: 1120 us
  waiting for transfers between devices  690 us (62%)
  blocking collectives  323 us (29%)
  starting transfers between devices  59.7 us (5%)
  between operations  16.2 us (1%)
  matrix products  14.3 us (1%)
    all_gather x1, waiting for transfers between devices, local(): lax.all_gather(gate_weight, 'dp', axis=0, tiled=True)  486 us
    unnamed x23, waiting for transfers between devices  172 us
    unnamed x1, blocking collectives  167 us
    psum x1, blocking collectives, local(): all_tokens = lax.psum(jnp.sum(counts).astype(jnp.float32), 'dp')  156 us
    unnamed x20, starting transfers between devices  59.6 us
    all_gather x1, waiting for transfers between devices, local(): group = lax.all_gather(tokens, 'mp', axis=0, tiled=True)  31.7 us
  transfers between devices with their start and end apart: 22, of which 3 were waited for; matrix products, arithmetic and copies ran while one was open for 17% of the time, Pallas kernels for 0%

commit v1 on v0

v1 whole, which is shorter than its diff:
```python
import jax
import jax.numpy as jnp
from jax import lax
from jax.sharding import Mesh, PartitionSpec as P

EMA_DECAY = 0.8
NZ, NY = 8, 4
DP = ("z", "y", "xl")
MP = ("xh", "c")


def swap(x, axis):
    return lax.ppermute(x, axis, [(0, 1), (1, 0)])


def block_grams(rows, blk):
    stacked = rows.reshape(rows.shape[0], -1, blk)
    grams = jnp.einsum("tkb,tkc->kbc", stacked, stacked, preferred_element_type=jnp.float32)
    return grams.reshape(-1, blk)


def scatter_strips(statistic, owner_map, send_type):
    blk = statistic.shape[-1]
    n_dp = owner_map.shape[0]
    strips = statistic.astype(send_type).reshape(n_dp, -1, blk)
    height = strips.shape[1]
    slots = jnp.take(strips, owner_map, axis=0).reshape(NZ, NY, 2, height, blk)
    got = lax.all_to_all(slots, "y", 1, 1, tiled=False)
    part = jnp.sum(got.astype(jnp.float32), axis=1)
    got = lax.all_to_all(part, "xl", 1, 1, tiled=False)
    part = jnp.sum(got, axis=1)
    got = lax.all_to_all(part, "z", 0, 0, tiled=False)
    return jnp.sum(got, axis=0)


def local(tokens, gate_weight, grad_hidden, counts, sampled, owner_map, input_factor, grad_factor):
    blk = input_factor.shape[2]
    n_dp = owner_map.shape[0]
    xl = lax.axis_index("xl")
    c = lax.axis_index("c")
    mp = lax.axis_index("xh") * 2 + c
    panel = gate_weight.shape[1]
    half_blocks = (panel // blk + 1) // 2
    width = half_blocks * blk
    step = panel - width

    mine = lax.dynamic_slice_in_dim(gate_weight, xl * step, width, 1)
    theirs = lax.dynamic_slice_in_dim(gate_weight, (1 - xl) * step, width, 1)
    got = swap(theirs, "xl")
    first = jnp.where(xl == 0, mine, got)
    second = jnp.where(xl == 0, got, mine)
    shard = jnp.concatenate([first, second], axis=0)
    weight = lax.all_gather(shard, ("z", "y"), axis=0, tiled=True)

    all_counts = lax.all_gather(counts, DP, axis=0, tiled=True)
    all_tokens = jnp.sum(all_counts).astype(jnp.float32)
    other_count = swap(counts, "xl")[0]

    group = lax.all_gather(tokens, MP, axis=0, tiled=True)
    tok_dev = group.shape[0]
    part = lax.dynamic_slice_in_dim(group, c * (tok_dev // 2), tok_dev // 2, 0)
    other_part = swap(part, "xl")
    other_rest = swap(other_part, "c")
    other = jnp.where(
        c == 0,
        jnp.concatenate([other_part, other_rest], axis=0),
        jnp.concatenate([other_rest, other_part], axis=0),
    )
    slot = lax.iota(jnp.int32, tok_dev)
    live_own = slot < counts[0]
    live_other = slot < other_count

    region = tokens.shape[1] // (2 * 2)
    own_columns = lax.dynamic_slice_in_dim(group, mp * region, region, 1)
    own_columns = jnp.where(live_own[:, None], own_columns, jnp.zeros((), jnp.bfloat16))
    input_stat = scatter_strips(block_grams(own_columns, blk), owner_map, jnp.float32)
    input_ema = EMA_DECAY * input_factor + (1.0 - EMA_DECAY) * (input_stat / all_tokens).reshape(
        input_factor.shape
    )

    def gate(rows, live):
        sums = jnp.dot(rows, weight, preferred_element_type=jnp.float32)
        return jnp.where(live[:, None], jax.nn.silu(sums), 0.0).astype(jnp.bfloat16)

    act_other = gate(other, live_other)
    act_own = gate(group, live_own)
    away = lax.dynamic_slice_in_dim(act_other, xl * (width - step), step, 1)
    back = swap(away, "xl")
    activation = jnp.where(
        xl == 0,
        jnp.concatenate([act_own, back], axis=1),
        jnp.concatenate([back, act_own], axis=1),
    )

    pick = (sampled[:, None] == slot[None, :]).astype(jnp.bfloat16)
    picked = jnp.dot(pick, activation, preferred_element_type=jnp.float32)
    grad_rows = (grad_hidden.astype(jnp.float32) * picked).astype(jnp.bfloat16)
    grad_stat = scatter_strips(block_grams(grad_rows, blk), owner_map, jnp.float32)
    sample_total = jnp.float32(grad_hidden.shape[0] * n_dp)
    grad_ema = EMA_DECAY * grad_factor + (1.0 - EMA_DECAY) * (grad_stat / sample_total).reshape(
        grad_factor.shape
    )
    return (activation, input_ema, grad_ema)


def solution(mesh):
    fine = Mesh(mesh.devices.reshape(NZ, NY, 2, 2, 2), ("z", "y", "xl", "xh", "c"))
    in_specs = (
        P(DP + MP, None),
        P(DP, MP),
        P(DP, MP),
        P(DP),
        P(DP),
        P(),
        P(MP, DP, None),
        P(MP, DP, None),
    )
    out_specs = (P(DP, MP), P(MP, DP, None), P(MP, DP, None))
    return jax.shard_map(local, mesh=fine, in_specs=in_specs, out_specs=out_specs, check_vma=False)
```

time: 1120 us -> 275 us (0.25)
  waiting for transfers between devices: 690 us -> 173 us
  blocking collectives: 323 us -> 18.7 us
  starting transfers between devices: 59.7 us -> 30.6 us
    all_gather x2, waiting for transfers between devices: 518 us -> 86.3 us  [the longest x1 59.4 us: local(): weight = lax.all_gather(shard, ('z', 'y'), axis=0, tiled=True)]
    unnamed x23 -> x2, waiting for transfers between devices: 172 us -> 0.7 us
    psum x1 -> x0, blocking collectives: 156 us -> none  [local(): all_tokens = lax.psum(jnp.sum(counts).astype(jnp.float32), 'dp')]
    unnamed x1, blocking collectives: 167 us -> 18.7 us
    unnamed x20 -> x0, starting transfers between devices: 59.6 us -> none
    ppermute x0 -> x5, waiting for transfers between devices: none -> 48.3 us  [swap(): return lax.ppermute(x, axis, [(0, 1), (1, 0)])]
    all_to_all x0 -> x6, waiting for transfers between devices: none -> 38.1 us  [the longest x2 21.4 us: scatter_strips(): got = lax.all_to_all(slots, 'y', 1, 1, tiled=False)]
    all_to_all x0 -> x6, starting transfers between devices: none -> 23.6 us  [the longest x2 8.95 us: scatter_strips(): got = lax.all_to_all(part, 'z', 0, 0, tiled=False)]
  transfers between devices with their start and end apart: 22 -> 13, of which waited for: 3 -> 10; matrix products, arithmetic and copies ran while one was open for 17% -> 12% of each run, Pallas kernels for 0% -> 0%
where the time goes in v1:
time: 275 us; the launch traced here: 274 us
  waiting for transfers between devices  173 us (63%)
  starting transfers between devices  30.6 us (11%)
  blocking collectives  18.7 us (7%)
  matrix products  15.9 us (6%)
  between operations  15.7 us (6%)
  other arithmetic  10.8 us (4%)
  local copies, waits for them, and re-layouts  8.78 us (3%)
    all_gather x1, waiting for transfers between devices, local(): weight = lax.all_gather(shard, ('z', 'y'), axis=0, tiled=True)  59.4 us
    ppermute x5, waiting for transfers between devices, swap(): return lax.ppermute(x, axis, [(0, 1), (1, 0)])  48.3 us
    all_gather x1, waiting for transfers between devices, local(): group = lax.all_gather(tokens, MP, axis=0, tiled=True)  26.9 us
    all_to_all x2, waiting for transfers between devices, scatter_strips(): got = lax.all_to_all(slots, 'y', 1, 1, tiled=False)  21.4 us
    unnamed x1, blocking collectives  18.7 us
    all_to_all x2, waiting for transfers between devices, scatter_strips(): got = lax.all_to_all(part, 'z', 0, 0, tiled=False)  16.7 us
    dot_general x2, matrix products, gate(): sums = jnp.dot(rows, weight, preferred_element_type=jnp.float32)  14.3 us
    all_to_all x2, starting transfers between devices, scatter_strips(): got = lax.all_to_all(part, 'z', 0, 0, tiled=False)  8.95 us
  transfers between devices with their start and end apart: 13, of which 10 were waited for; matrix products, arithmetic and copies ran while one was open for 12% of the time, Pallas kernels for 0%

profile of v1, /device:TPU:4, one launch (start us, length us, event | category | flops | bytes accessed | tf_op | source)
XLA Modules:
  0.0 273.9 jit_solution(10999463550665802109)
XLA Ops:
  7.2 0.7 all-gather.5.cloned.1.call-update
  8.0 0.9 constant_dynamic-slice_fusion.1
  8.9 1.3 collective-permute-start
  10.2 5.2 %collective-permute-done = bf16[80,1152]{1,0:T(8,128)(2,1)S(1)} collective-permute-done((bf16[80,1152]{1,0:T(8,128)(2,1)S(1)}, bf16[80,1152]{1,0:T(8,128)(2,1)S(1)}, u32[]{:S(2)}, u32[]{:S(2)}) %collective-permute-start) | collective-permute-done | bytes 184352 | tf_op jit(solution)/shard_map/ppermute | solution.py:13
  15.4 1.0 broadcast_select_fusion.1
  16.4 0.8 pad_maximum_fusion
  17.2 26.9 %all-gather.5.cloned.1.call-done = bf16[288,5120]{1,0:T(8,128)(2,1)} async-done(((bf16[72,5120]{1,0:T(8,128)(2,1)}), bf16[288,5120]{1,0:T(8,128)(2,1)}) %all-gather.5.cloned.1.call-update) | async-done | bytes 2949136 | tf_op jit(solution)/shard_map/all_gather | solution.py:59
  44.1 1.5 constant_dynamic-slice_fusion
  45.6 2.4 collective-permute-start.2
  48.9 31.9 %collective-permute-done.2 = bf16[144,5120]{1,0:T(8,128)(2,1)} collective-permute-done((bf16[144,5120]{1,0:T(8,128)(2,1)S(1)}, bf16[144,5120]{1,0:T(8,128)(2,1)}, u32[]{:S(2)}, u32[]{:S(2)}) %collective-permute-start.2) | collective-permute-done | bytes 1474592 | tf_op jit(solution)/shard_map/ppermute | solution.py:13
  80.8 1.3 dynamic-slice_select_fusion
  82.1 0.6 copy.39
  82.7 0.5 fusion.15
  83.3 0.6 gather_fusion
  84.0 1.3 copy_select_fusion.1
  85.2 4.3 %all-to-all-start = ((f32[8,4,2,20,128]{4,0,3,2,1:T(8,128)}), f32[8,4,2,20,128]{4,0,3,2,1:T(8,128)S(1)}, u32[]{:S(2)}, u32[]{:S(2)}) async-start(f32[8,4,2,20,128]{4,0,3,2,1:T(8,128)} %copy_select_fusion.1), calls=%async_computation | async-start | bytes 1310720 | tf_op jit(solution)/shard_map/all_to_all | solution.py:28
  89.5 1.8 collective-permute-start.1
  91.3 1.9 collective-permute-done.1
  93.1 0.6 iota_compare_fusion.2
  93.8 7.3 %all-to-all-done = f32[8,4,2,20,128]{4,0,3,2,1:T(8,128)S(1)} async-done(((f32[8,4,2,20,128]{4,0,3,2,1:T(8,128)}), f32[8,4,2,20,128]{4,0,3,2,1:T(8,128)S(1)}, u32[]{:S(2)}, u32[]{:S(2)}) %all-to-all-start) | async-done | bytes 655392 | tf_op jit(solution)/shard_map/all_to_all | solution.py:28
  101.1 0.7 reduce_sum.63
  101.8 3.4 %all-to-all-start.1 = ((f32[8,2,20,128]{3,0,2,1:T(8,128)}), f32[8,2,20,128]{3,0,2,1:T(8,128)S(1)}, u32[]{:S(2)}, u32[]{:S(2)}) async-start(f32[8,2,20,128]{3,0,2,1:T(8,128)} %reduce_sum.63), calls=%async_computation.1 | async-start | bytes 327680 | tf_op jit(solution)/shard_map/all_to_all | solution.py:30
  105.2 59.4 %all-gather.3.cloned.1.call-done = bf16[5120,1152]{1,0:T(8,128)(2,1)} async-done(((bf16[160,1152]{1,0:T(8,128)(2,1)}), bf16[5120,1152]{1,0:T(8,128)(2,1)}) %all-gather.3.cloned.1.call-update) | async-done | bytes 11796496 | tf_op jit(solution)/shard_map/all_gather | solution.py:53
  164.6 10.2 %fusion.14 = (f32[288,1152]{1,0:T(8,128)S(1)}, f32[288,1152]{1,0:T(8,128)S(1)}) fusion(bf16[5120,1152]{1,0:T(8,128)(2,1)} %all-gather.3.cloned.1.call-done, bf16[144,5120]{1,0:T(8,128)(2,1)} %collective-permute-done.3, bf16[144,5120]{1,0:T(8,128)(2,1)} %collective-permute-done.2, pred[]{:T(512)S(6)} %eq.22), kind=kOutput, calls=%fused_computation.41 | convolution fusion | flops 3410989056 | bytes 17399808 | tf_op jit(solution)/shard_map/dot_general | solution.py:82
  175.2 1.4 collective-permute-start.4
  176.6 4.1 %select_convert_fusion = bf16[288,1152]{1,0:T(8,128)(2,1)S(1)} fusion(bf16[288,5120]{1,0:T(8,128)(2,1)S(1)} %copy-done.1, bf16[5120,1152]{1,0:T(8,128)(2,1)S(1)} %copy-done.6, pred[288]{0:T(512)(128)(4,1)S(1)} %iota_compare_fusion.3), kind=kOutput, calls=%fused_computation.13 | convolution fusion | flops 3399376896 | bytes 15409440 | tf_op jit(solution)/shard_map/dot_general | solution.py:82
  180.8 9.4 %collective-permute-done.4 = bf16[288,1024]{1,0:T(8,128)(2,1)S(1)} collective-permute-done((bf16[288,1024]{1,0:T(8,128)(2,1)S(1)}, bf16[288,1024]{1,0:T(8,128)(2,1)S(1)}, u32[]{:S(2)}, u32[]{:S(2)}) %collective-permute-start.4) | collective-permute-done | bytes 589856 | tf_op jit(solution)/shard_map/ppermute | solution.py:13
  190.5 1.0 copy-done
  191.5 0.5 fusion
  192.4 0.5 fusion.16
  193.0 0.7 gather_fusion.1
  193.6 1.7 copy_select_fusion
  195.4 3.5 %all-to-all-start.3 = ((f32[8,4,2,34,128]{4,0,3,2,1:T(8,128)}), f32[8,4,2,34,128]{4,0,3,2,1:T(8,128)S(1)}, u32[]{:S(2)}, u32[]{:S(2)}) async-start(f32[8,4,2,34,128]{4,0,3,2,1:T(8,128)} %copy_select_fusion), calls=%async_computation.3 | async-start | bytes 2228224 | tf_op jit(solution)/shard_map/all_to_all | solution.py:28
  198.9 0.6 copy.43
  199.6 14.1 %all-to-all-done.3 = f32[8,4,2,34,128]{4,0,3,2,1:T(8,128)S(1)} async-done(((f32[8,4,2,34,128]{4,0,3,2,1:T(8,128)}), f32[8,4,2,34,128]{4,0,3,2,1:T(8,128)S(1)}, u32[]{:S(2)}, u32[]{:S(2)}) %all-to-all-start.3) | async-done | bytes 1114144 | tf_op jit(solution)/shard_map/all_to_all | solution.py:28
  213.6 4.4 %all-to-all-start.2 = ((f32[8,20,128]{2,1,0:T(8,128)}), f32[8,20,128]{2,1,0:T(8,128)S(1)}, u32[]{:S(2)}, u32[]{:S(2)}) async-start(f32[8,20,128]{2,1,0:T(8,128)} %copy.43), calls=%async_computation.2 | async-start | bytes 196608 | tf_op jit(solution)/shard_map/all_to_all | solution.py:32
  218.0 0.8 reduce_sum.67
  218.8 7.9 %all-to-all-done.2 = f32[8,20,128]{2,1,0:T(8,128)S(1)} async-done(((f32[8,20,128]{2,1,0:T(8,128)}), f32[8,20,128]{2,1,0:T(8,128)S(1)}, u32[]{:S(2)}, u32[]{:S(2)}) %all-to-all-start.2) | async-done | bytes 81952 | tf_op jit(solution)/shard_map/all_to_all | solution.py:32
  226.7 3.4 %all-to-all-start.4 = ((f32[8,2,34,128]{3,0,2,1:T(8,128)}), f32[8,2,34,128]{3,0,2,1:T(8,128)S(1)}, u32[]{:S(2)}, u32[]{:S(2)}) async-start(f32[8,2,34,128]{3,0,2,1:T(8,128)} %reduce_sum.67), calls=%async_computation.4 | async-start | bytes 557056 | tf_op jit(solution)/shard_map/all_to_all | solution.py:30
  230.2 0.6 dynamic-slice
  230.8 0.8 dynamic-update-slice
  231.5 18.7 %all-reduce = s32[64]{0:T(128)S(1)} all-reduce(s32[64]{0:T(128)S(1)} %dynamic-update-slice), channel_id=1, replica_groups=mesh['z'=8,'y'=4,'xl'=2,'xh'=2,'c'=2] {'z','y','xl'}, use_global_device_ids=true, to_apply=%add | all-reduce | flops 64 | bytes 512
  250.3 0.6 reduce_sum.66
  251.6 0.7 copy.48
  252.3 4.6 %all-to-all-start.5 = ((f32[8,34,128]{2,1,0:T(8,128)}), f32[8,34,128]{2,1,0:T(8,128)S(1)}, u32[]{:S(2)}, u32[]{:S(2)}) async-start(f32[8,34,128]{2,1,0:T(8,128)} %copy.48), calls=%async_computation.5 | async-start | bytes 327680 | tf_op jit(solution)/shard_map/all_to_all | solution.py:32
  256.9 0.6 reshape_add_fusion.1
  257.5 8.8 %all-to-all-done.5 = f32[8,34,128]{2,1,0:T(8,128)S(1)} async-done(((f32[8,34,128]{2,1,0:T(8,128)}), f32[8,34,128]{2,1,0:T(8,128)S(1)}, u32[]{:S(2)}, u32[]{:S(2)}) %all-to-all-start.5) | async-done | bytes 139296 | tf_op jit(solution)/shard_map/all_to_all | solution.py:32
  266.4 0.6 reshape_add_fusion
  (42 shorter events, 1.6 us)
Async XLA Ops:
  7.2 36.9 %all-gather.5.cloned.1.call-start = ((), (), s32[]{:S(2)}) async-start(), calls=%async_computation.7 | async-start | bytes 3686400 | tf_op jit(solution)/shard_map/all_gather | solution.py:59
  7.9 156.7 %all-gather.3.cloned.1.call-start = ((), (), s32[]{:S(2)}) async-start(), calls=%async_computation.6 | async-start | bytes 12165120 | tf_op jit(solution)/shard_map/all_gather | solution.py:53
  8.9 6.5 %collective-permute-start = (bf16[80,1152]{1,0:T(8,128)(2,1)S(1)}, bf16[80,1152]{1,0:T(8,128)(2,1)S(1)}, u32[]{:S(2)}, u32[]{:S(2)}) collective-permute-start(bf16[80,1152]{1,0:T(8,128)(2,1)S(1)} %constant_dynamic-slice_fusion.1), channel_id=1, source_target_pairs={{0,4},{4,0},{1,5},{5,1},{2,6},{6,2},{3,7},{7,3},{8,12},{12,8},{9,1... | collective-permute-start | bytes 552968 | tf_op jit(solution)/shard_map/ppermute | solution.py:13
  17.2 31.5 %copy-start.7 = (s32[64]{0:T(128)S(1)}, s32[64]{0:T(128)}, u32[]{:S(2)}) copy-start(s32[64]{0:T(128)} %param.13) | copy-start | bytes 772
  45.6 35.2 %collective-permute-start.2 = (bf16[144,5120]{1,0:T(8,128)(2,1)S(1)}, bf16[144,5120]{1,0:T(8,128)(2,1)}, u32[]{:S(2)}, u32[]{:S(2)}) collective-permute-start(bf16[144,5120]{1,0:T(8,128)(2,1)S(1)} %constant_dynamic-slice_fusion), channel_id=1, source_target_pairs={{0,4},{4,0},{1,5},{5,1},{2,6},{6,2},{3,7},{7,3},{8,12},{12,8},{9,1... | collective-permute-start | bytes 4423688 | tf_op jit(solution)/shard_map/ppermute | solution.py:13
  80.8 24.4 %collective-permute-start.3 = (bf16[144,5120]{1,0:T(8,128)(2,1)}, bf16[144,5120]{1,0:T(8,128)(2,1)}, u32[]{:S(2)}, u32[]{:S(2)}) collective-permute-start(bf16[144,5120]{1,0:T(8,128)(2,1)} %collective-permute-done.2), channel_id=1, source_target_pairs={{0,1},{1,0},{2,3},{3,2},{4,5},{5,4},{6,7},{7,6},{8,9},{9,8},{10,11... | collective-permute-start | bytes 4423688 | tf_op jit(solution)/shard_map/ppermute | solution.py:13
  85.2 15.8 %all-to-all-start = ((f32[8,4,2,20,128]{4,0,3,2,1:T(8,128)}), f32[8,4,2,20,128]{4,0,3,2,1:T(8,128)S(1)}, u32[]{:S(2)}, u32[]{:S(2)}) async-start(f32[8,4,2,20,128]{4,0,3,2,1:T(8,128)} %copy_select_fusion.1), calls=%async_computation | async-start | bytes 1310720 | tf_op jit(solution)/shard_map/all_to_all | solution.py:28
  89.5 3.6 %collective-permute-start.1 = (s32[1]{0:T(128)}, s32[1]{0:T(128)}, u32[]{:S(2)}, u32[]{:S(2)}) collective-permute-start(s32[1]{0:T(128)} %param.11), channel_id=1, source_target_pairs={{0,4},{4,0},{1,5},{5,1},{2,6},{6,2},{3,7},{7,3},{8,12},{12,8},{9,1... | collective-permute-start | bytes 20 | tf_op jit(solution)/shard_map/ppermute | solution.py:13
  101.8 93.6 %all-to-all-start.1 = ((f32[8,2,20,128]{3,0,2,1:T(8,128)}), f32[8,2,20,128]{3,0,2,1:T(8,128)S(1)}, u32[]{:S(2)}, u32[]{:S(2)}) async-start(f32[8,2,20,128]{3,0,2,1:T(8,128)} %reduce_sum.63), calls=%async_computation.1 | async-start | bytes 327680 | tf_op jit(solution)/shard_map/all_to_all | solution.py:30
  164.6 12.0 %copy-start.6 = (bf16[5120,1152]{1,0:T(8,128)(2,1)S(1)}, bf16[5120,1152]{1,0:T(8,128)(2,1)}, u32[]{:S(2)}) copy-start(bf16[5120,1152]{1,0:T(8,128)(2,1)} %all-gather.3.cloned.1.call-done) | copy-start | bytes 35389444
  174.8 1.8 copy-start.1
  175.2 15.0 %collective-permute-start.4 = (bf16[288,1024]{1,0:T(8,128)(2,1)S(1)}, bf16[288,1024]{1,0:T(8,128)(2,1)S(1)}, u32[]{:S(2)}, u32[]{:S(2)}) collective-permute-start(bf16[288,1024]{1,0:T(8,128)(2,1)S(1)} %fusion.9), channel_id=1, source_target_pairs={{0,4},{4,0},{1,5},{5,1},{2,6},{6,2},{3,7},{7,3},{8,12},{12,8},{9,1... | collective-permute-start | bytes 1769480 | tf_op jit(solution)/shard_map/ppermute | solution.py:13
  180.7 10.8 %copy-start.2 = (bf16[128,2176]{1,0:T(8,128)(2,1)S(1)}, bf16[128,2176]{1,0:T(8,128)(2,1)}, u32[]{:S(2)}) copy-start(bf16[128,2176]{1,0:T(8,128)(2,1)} %param.10) | copy-start | bytes 1671172
  180.8 10.8 %copy-start.5 = (s32[128]{0:T(128)S(1)}, s32[128]{0:T(128)}, u32[]{:S(2)}) copy-start(s32[128]{0:T(128)} %param.12) | copy-start | bytes 1540
  190.5 1.0 copy-start
  195.4 18.3 %all-to-all-start.3 = ((f32[8,4,2,34,128]{4,0,3,2,1:T(8,128)}), f32[8,4,2,34,128]{4,0,3,2,1:T(8,128)S(1)}, u32[]{:S(2)}, u32[]{:S(2)}) async-start(f32[8,4,2,34,128]{4,0,3,2,1:T(8,128)} %copy_select_fusion), calls=%async_computation.3 | async-start | bytes 2228224 | tf_op jit(solution)/shard_map/all_to_all | solution.py:28
  198.9 31.3 %copy-start.8 = (u32[256]{0:T(256)S(1)}, u32[256]{0:T(256)}, u32[]{:S(2)}) copy-start(u32[256]{0:T(256)} %constant.84) | copy-start | bytes 3076
  213.6 13.1 %all-to-all-start.2 = ((f32[8,20,128]{2,1,0:T(8,128)}), f32[8,20,128]{2,1,0:T(8,128)S(1)}, u32[]{:S(2)}, u32[]{:S(2)}) async-start(f32[8,20,128]{2,1,0:T(8,128)} %copy.43), calls=%async_computation.2 | async-start | bytes 196608 | tf_op jit(solution)/shard_map/all_to_all | solution.py:32
  218.0 38.9 %copy-start.4 = (f32[1,20,128]{2,0,1:T(1,128)S(1)}, f32[1,20,128]{2,0,1:T(1,128)}, u32[]{:S(2)}) copy-start(f32[1,20,128]{2,0,1:T(1,128)} %param.14) | copy-start | bytes 30724
  218.8 47.6 %copy-start.3 = (f32[1,34,128]{2,0,1:T(1,128)S(1)}, f32[1,34,128]{2,0,1:T(1,128)}, u32[]{:S(2)}) copy-start(f32[1,34,128]{2,0,1:T(1,128)} %param.15) | copy-start | bytes 52228
  226.7 24.9 %all-to-all-start.4 = ((f32[8,2,34,128]{3,0,2,1:T(8,128)}), f32[8,2,34,128]{3,0,2,1:T(8,128)S(1)}, u32[]{:S(2)}, u32[]{:S(2)}) async-start(f32[8,2,34,128]{3,0,2,1:T(8,128)} %reduce_sum.67), calls=%async_computation.4 | async-start | bytes 557056 | tf_op jit(solution)/shard_map/all_to_all | solution.py:30
  252.3 14.0 %all-to-all-start.5 = ((f32[8,34,128]{2,1,0:T(8,128)}), f32[8,34,128]{2,1,0:T(8,128)S(1)}, u32[]{:S(2)}, u32[]{:S(2)}) async-start(f32[8,34,128]{2,1,0:T(8,128)} %copy.48), calls=%async_computation.5 | async-start | bytes 327680 | tf_op jit(solution)/shard_map/all_to_all | solution.py:32
Sparse Core Ops, SparseCore 0:
  9.8 34.2 all-gather.4
  46.7 117.8 all-gather.2
